TPU v7x, 32 devices: a whole 2x2x4 slice. The times are simulated.
32 devices in a mesh: gx: 4 (over y, core), gy: 8 (over z, x).
Axes of the slice: x: 2, y: 2, z: 4, core: 2. Of those that a mesh axis runs over, the one named last changes fastest.
Arguments:
- positions: float32 [3, 1024, 4096], P(None, 'gx', 'gy'), may hold values from -6 to 6
- velocity: float32 [3, 1024, 4096], P(None, 'gx', 'gy'), may hold values from -3 to 3
- stiffness: float32 [1024, 4096], P('gx', 'gy'), may hold values from 0.5 to 4
- send_tiles: int32 [4, 8, 128], P('gx', 'gy'), may hold values from -1 to 1023, as said below
- pair_tiles: int32 [4, 8, 2, 256], P('gx', 'gy'), may hold values from -1 to 127, as said below
Outputs:
- new_positions: float32 [3, 1024, 4096], P(None, 'gx', 'gy')
- new_velocity: float32 [3, 1024, 4096], P(None, 'gx', 'gy')
Inputs may be any that keep to these rules, and one draw needn't show every extreme that they name: `send_tiles`: entry o * 4 + k of a device names the patch tile in slot k towards owner o, -1 marking an empty slot; the filled slots towards an owner come first, and some owner receives all 4 slots filled from every device. `pair_tiles`: at each owner, column m is a face-pair tile: its two rows name two different filled received slots, slot s * 4 + k being slot k sent to this owner by owner s. Unused columns hold -1 in both rows and follow the used ones; some owner uses all 256 columns.
All inputs are finite; a program needn't handle non-finite values.
Results may differ from a plain program's by a relative error of at most 0.0003.
Values sent between devices are 32-bit elements; how exact they have to be, the bound alone decides.
A program may use at most 64 MiB of HBM per device.

v0:
```python
import jax
import jax.numpy as jnp
from jax import lax
from jax.sharding import PartitionSpec as P

TILE = 128
STEPS = 2


time_step = 0.1
damping = 0.2
hardening = 0.1
bend_gain = 0.02
contact_gain = 0.25
inverse_width = 0.5
block_rows = 32


def extended(cells, sides, width):
    for axis, dim in sides:
        count = lax.axis_size(axis)
        ends = count - 1
        head = lax.slice_in_dim(cells, 0, width, axis=dim)
        tail = lax.slice_in_dim(cells, cells.shape[dim] - width, cells.shape[dim], axis=dim)
        cells = jnp.concatenate(
            [
                lax.ppermute(tail, axis, [(i, (i + 1) % count) for i in range(ends)]),
                cells,
                lax.ppermute(head, axis, [((i + 1) % count, i) for i in range(ends)]),
            ],
            axis=dim,
        )
    return cells


def neighbours(padded):
    return (padded[:, 2:, 1:-1], padded[:, :-2, 1:-1], padded[:, 1:-1, 2:], padded[:, 1:-1, :-2])


def membrane(padded):
    center = padded[:, 1:-1, 1:-1]
    result = jnp.zeros(center.shape, jnp.float32)
    for beside in neighbours(padded):
        offset = beside - center
        result = result + offset * (
            1.0 + hardening * jnp.sum(offset * offset, axis=0, keepdims=True)
        )
    return result


def laplace(padded):
    beside_all = neighbours(padded)
    return (
        beside_all[0]
        + beside_all[1]
        + (beside_all[2] + beside_all[3])
        - 4.0 * padded[:, 1:-1, 1:-1]
    )


def pair_block(near, far, active):
    offset = near[:, :, :, None] - far[:, :, None, :]
    weight = (
        contact_gain
        * jnp.exp(-inverse_width * jnp.sum(offset * offset, axis=0))
        * active[:, None, None]
    )
    push = weight[None] * offset
    return (jnp.sum(push, axis=3), -jnp.sum(push, axis=2))


def pair_forces(received, paired):
    first = paired[0]
    second = paired[1]
    active = (first >= 0).astype(jnp.float32)
    first_row = jnp.maximum(first, 0)
    second_row = jnp.maximum(second, 0)
    near = jnp.take(received, first_row, axis=1)
    far = jnp.take(received, second_row, axis=1)
    number = paired.shape[1]
    groups = number // block_rows

    def split_blocks(values):
        return jnp.moveaxis(values.reshape(3, groups, block_rows, values.shape[2]), 1, 0)

    def run_block(items):
        return pair_block(items[0], items[1], items[2])

    near_out, far_out = lax.map(
        run_block, (split_blocks(near), split_blocks(far), active.reshape(groups, block_rows))
    )
    near_force = jnp.moveaxis(near_out, 0, 1).reshape(3, number, received.shape[2])
    far_force = jnp.moveaxis(far_out, 0, 1).reshape(3, number, received.shape[2])
    return (near_force, far_force, first_row, second_row, active)


def internal(positions, stiffness):
    wide = extended(positions, (("gx", 1), ("gy", 2)), 2)
    padded = wide[:, 1:-1, 1:-1]
    row_count = positions.shape[1]
    col_count = positions.shape[2]
    row_index = lax.axis_index("gx") * row_count + jnp.arange(row_count + 2) - 1
    col_index = lax.axis_index("gy") * col_count + jnp.arange(col_count + 2) - 1
    row_inside = (row_index >= 0) & (row_index < row_count * lax.axis_size("gx"))
    col_inside = (col_index >= 0) & (col_index < col_count * lax.axis_size("gy"))
    inside = (row_inside[:, None] & col_inside[None, :]).astype(jnp.float32)
    curve = laplace(wide) * inside[None]
    bend = laplace(curve)
    return stiffness[None] * membrane(padded) - bend_gain * bend


def contact_force(positions, route, paired):
    flat = positions.reshape(3, -1, TILE)
    filled = (route >= 0).astype(jnp.float32)
    sent = jnp.take(flat, jnp.maximum(route, 0), axis=1) * filled[None, :, None]
    received = lax.all_to_all(sent, ("gx", "gy"), split_axis=1, concat_axis=1, tiled=True)
    near_force, far_force, first_row, second_row, active = pair_forces(received, paired)
    slot_ids = jnp.arange(received.shape[1])
    first_hot = (first_row[:, None] == slot_ids[None, :]).astype(jnp.float32) * active[:, None]
    second_hot = (second_row[:, None] == slot_ids[None, :]).astype(jnp.float32) * active[:, None]
    slot_force = jnp.einsum("ps,cpt->cst", first_hot, near_force, precision=lax.Precision.HIGHEST)
    slot_force = slot_force + jnp.einsum(
        "ps,cpt->cst", second_hot, far_force, precision=lax.Precision.HIGHEST
    )
    returned = lax.all_to_all(slot_force, ("gx", "gy"), split_axis=1, concat_axis=1, tiled=True)
    tile_ids = jnp.arange(flat.shape[1])
    route_hot = (route[:, None] == tile_ids[None, :]).astype(jnp.float32)
    tile_force = jnp.einsum("sn,cst->cnt", route_hot, returned, precision=lax.Precision.HIGHEST)
    return tile_force.reshape(positions.shape)


def local(positions, velocity, stiffness, send_tiles, pair_tiles):
    route = send_tiles.reshape(-1)
    paired = pair_tiles.reshape(2, -1)
    for repeat in range(STEPS):
        force = internal(positions, stiffness) + contact_force(positions, route, paired)
        velocity = velocity + time_step * (force - damping * velocity)
        positions = positions + time_step * velocity
    return (positions, velocity)


def solution(mesh):
    return jax.shard_map(
        local,
        mesh=mesh,
        in_specs=(
            P(None, "gx", "gy"),
            P(None, "gx", "gy"),
            P("gx", "gy"),
            P("gx", "gy", None),
            P("gx", "gy", None, None),
        ),
        out_specs=(P(None, "gx", "gy"), P(None, "gx", "gy")),
        check_vma=False,
    )
```

profile of v0, /device:TPU:0, one launch (start us, length us, event | category | flops | bytes accessed | tf_op | source)
XLA Modules:
  0.0 292.1 jit_solution(9458938031456782126)
XLA Ops:
  1.5 2.4 collective-permute-start.1
  6.5 1.4 reshape.231
  7.9 2.4 copy.65
  10.3 2.5 gather_fusion
  13.9 9.2 %all-to-all-start = ((f32[3,128,128]{2,0,1:T(4,128)}), f32[3,128,128]{2,0,1:T(4,128)S(1)}, u32[]{:S(2)}, u32[]{:S(2)}) async-start(f32[3,128,128]{2,0,1:T(4,128)} %bitcast_multiply_fusion.1), calls=%async_computation | async-start | bytes 524288 | tf_op jit(solution)/shard_map/all_to_all | solution.py:116
  24.6 3.7 %collective-permute-start.3 = (f32[3,260,2]{2,1,0:T(8,128)}, f32[3,260,2]{2,1,0:T(8,128)S(1)}, u32[]{:S(2)}, u32[]{:S(2)}) collective-permute-start(f32[3,260,2]{2,1,0:T(8,128)} %get-tuple-element.172), channel_id=1, source_target_pairs={{0,1},{1,2},{2,3},{3,4},{4,5},{5,6},{6,7},{8,9},{9,10},{10,11},{11... | collective-permute-start | bytes 18728 | tf_op jit(solution)/shard_map/ppermute | solution.py:27
  29.7 17.2 %collective-permute-done.3 = f32[3,260,2]{2,1,0:T(8,128)S(1)} collective-permute-done((f32[3,260,2]{2,1,0:T(8,128)}, f32[3,260,2]{2,1,0:T(8,128)S(1)}, u32[]{:S(2)}, u32[]{:S(2)}) %collective-permute-start.3) | collective-permute-done | bytes 6272 | tf_op jit(solution)/shard_map/ppermute | solution.py:27
  47.7 1.4 multiply_reduce_fusion.7
  50.7 2.1 pad_maximum_fusion.1
  57.5 57.8 %while.24 = (s32[]{:T(128)}, f32[8,3,32,128]{3,2,0,1:T(8,128)S(1)}, f32[8,3,32,128]{3,2,0,1:T(8,128)S(1)}, f32[8,3,32,128]{3,2,0,1:T(8,128)}, f32[8,3,32,128]{3,...) while((s32[]{:T(128)}, f32[8,3,32,128]{3,2,0,1:T(8,128)S(1)}, f32[8,3,32,128]{3,2,0,1:T(8,128)S(1)}, ...), condition=%wide.region_8.11_spmd, body=%wide.region_4.10_spmd.sunk | while | flops 11522082 | bytes 9077221 | solution.py:89
  58.4 2.1 fusion.92
  60.8 3.9 %fusion.94 = (f32[3,32,128]{2,1,0:T(8,128)S(1)}, f32[3,32,128]{2,1,0:T(8,128)S(1)}) fusion(f32[32,128,128]{2,1,0:T(8,128)S(1)} %exponential_multiply_fusion.4, f32[3,32,128]{2,1,0:T(8,128)S(1)} %dynamic-slice_bitcast_fusion.8, f32[3,32,128]{2,1,0:T(8,128)S(1)} %dynamic-slice_bitcast_fusion.9), kind=kLoop, calls=%fused_computation.8.clone.1 | loop fusion | flops 6266880 | bytes 2293760 | tf_op jit(solution)/shard_map/while/body/eval_jaxpr/reduce_sum | solution.py:69
  65.6 2.1 fusion.92
  68.0 3.9 %fusion.94 = (f32[3,32,128]{2,1,0:T(8,128)S(1)}, f32[3,32,128]{2,1,0:T(8,128)S(1)}) fusion(f32[32,128,128]{2,1,0:T(8,128)S(1)} %exponential_multiply_fusion.4, f32[3,32,128]{2,1,0:T(8,128)S(1)} %dynamic-slice_bitcast_fusion.8, f32[3,32,128]{2,1,0:T(8,128)S(1)} %dynamic-slice_bitcast_fusion.9), kind=kLoop, calls=%fused_computation.8.clone.1 | loop fusion | flops 6266880 | bytes 2293760 | tf_op jit(solution)/shard_map/while/body/eval_jaxpr/reduce_sum | solution.py:69
  72.8 2.1 fusion.92
  75.2 3.9 %fusion.94 = (f32[3,32,128]{2,1,0:T(8,128)S(1)}, f32[3,32,128]{2,1,0:T(8,128)S(1)}) fusion(f32[32,128,128]{2,1,0:T(8,128)S(1)} %exponential_multiply_fusion.4, f32[3,32,128]{2,1,0:T(8,128)S(1)} %dynamic-slice_bitcast_fusion.8, f32[3,32,128]{2,1,0:T(8,128)S(1)} %dynamic-slice_bitcast_fusion.9), kind=kLoop, calls=%fused_computation.8.clone.1 | loop fusion | flops 6266880 | bytes 2293760 | tf_op jit(solution)/shard_map/while/body/eval_jaxpr/reduce_sum | solution.py:69
  80.0 2.1 fusion.92
  82.4 3.9 %fusion.94 = (f32[3,32,128]{2,1,0:T(8,128)S(1)}, f32[3,32,128]{2,1,0:T(8,128)S(1)}) fusion(f32[32,128,128]{2,1,0:T(8,128)S(1)} %exponential_multiply_fusion.4, f32[3,32,128]{2,1,0:T(8,128)S(1)} %dynamic-slice_bitcast_fusion.8, f32[3,32,128]{2,1,0:T(8,128)S(1)} %dynamic-slice_bitcast_fusion.9), kind=kLoop, calls=%fused_computation.8.clone.1 | loop fusion | flops 6266880 | bytes 2293760 | tf_op jit(solution)/shard_map/while/body/eval_jaxpr/reduce_sum | solution.py:69
  87.3 2.1 fusion.92
  89.7 3.9 %fusion.94 = (f32[3,32,128]{2,1,0:T(8,128)S(1)}, f32[3,32,128]{2,1,0:T(8,128)S(1)}) fusion(f32[32,128,128]{2,1,0:T(8,128)S(1)} %exponential_multiply_fusion.4, f32[3,32,128]{2,1,0:T(8,128)S(1)} %dynamic-slice_bitcast_fusion.8, f32[3,32,128]{2,1,0:T(8,128)S(1)} %dynamic-slice_bitcast_fusion.9), kind=kLoop, calls=%fused_computation.8.clone.1 | loop fusion | flops 6266880 | bytes 2293760 | tf_op jit(solution)/shard_map/while/body/eval_jaxpr/reduce_sum | solution.py:69
  94.5 2.1 fusion.92
  96.9 3.9 %fusion.94 = (f32[3,32,128]{2,1,0:T(8,128)S(1)}, f32[3,32,128]{2,1,0:T(8,128)S(1)}) fusion(f32[32,128,128]{2,1,0:T(8,128)S(1)} %exponential_multiply_fusion.4, f32[3,32,128]{2,1,0:T(8,128)S(1)} %dynamic-slice_bitcast_fusion.8, f32[3,32,128]{2,1,0:T(8,128)S(1)} %dynamic-slice_bitcast_fusion.9), kind=kLoop, calls=%fused_computation.8.clone.1 | loop fusion | flops 6266880 | bytes 2293760 | tf_op jit(solution)/shard_map/while/body/eval_jaxpr/reduce_sum | solution.py:69
  101.7 2.1 fusion.92
  104.1 3.9 %fusion.94 = (f32[3,32,128]{2,1,0:T(8,128)S(1)}, f32[3,32,128]{2,1,0:T(8,128)S(1)}) fusion(f32[32,128,128]{2,1,0:T(8,128)S(1)} %exponential_multiply_fusion.4, f32[3,32,128]{2,1,0:T(8,128)S(1)} %dynamic-slice_bitcast_fusion.8, f32[3,32,128]{2,1,0:T(8,128)S(1)} %dynamic-slice_bitcast_fusion.9), kind=kLoop, calls=%fused_computation.8.clone.1 | loop fusion | flops 6266880 | bytes 2293760 | tf_op jit(solution)/shard_map/while/body/eval_jaxpr/reduce_sum | solution.py:69
  109.0 2.1 fusion.92
  111.3 3.9 %fusion.94 = (f32[3,32,128]{2,1,0:T(8,128)S(1)}, f32[3,32,128]{2,1,0:T(8,128)S(1)}) fusion(f32[32,128,128]{2,1,0:T(8,128)S(1)} %exponential_multiply_fusion.4, f32[3,32,128]{2,1,0:T(8,128)S(1)} %dynamic-slice_bitcast_fusion.8, f32[3,32,128]{2,1,0:T(8,128)S(1)} %dynamic-slice_bitcast_fusion.9), kind=kLoop, calls=%fused_computation.8.clone.1 | loop fusion | flops 6266880 | bytes 2293760 | tf_op jit(solution)/shard_map/while/body/eval_jaxpr/reduce_sum | solution.py:69
  118.0 6.2 %all-to-all-start.1 = ((f32[3,128,128]{2,0,1:T(4,128)}), f32[3,128,128]{2,0,1:T(4,128)S(1)}, u32[]{:S(2)}, u32[]{:S(2)}) async-start(f32[3,128,128]{2,0,1:T(4,128)} %copy.74), calls=%async_computation.1 | async-start | bytes 524288 | tf_op jit(solution)/shard_map/all_to_all | solution.py:125
  124.3 7.1 %fusion.14 = f32[3,258,514]{2,1,0:T(8,128)} fusion(f32[3,260,516]{2,1,0:T(8,128)} %pad_maximum_fusion.1, f32[3,260,514]{2,1,0:T(8,128)} %copy-done.4, f32[3,260,514]{2,1,0:T(8,128)} %copy-done.3, f32[258,514]{1,0:T(8,128)S(1)} %and_convert_fusion), kind=kLoop, calls=%fused_computation.40 | loop fusion | flops 2387016 | bytes 10078512 | tf_op jit(solution)/shard_map/mul | solution.py:107
  131.4 3.3 %all-to-all-done.1 = f32[3,128,128]{2,0,1:T(4,128)S(1)} async-done(((f32[3,128,128]{2,0,1:T(4,128)}), f32[3,128,128]{2,0,1:T(4,128)S(1)}, u32[]{:S(2)}, u32[]{:S(2)}) %all-to-all-start.1) | async-done | bytes 196640 | tf_op jit(solution)/shard_map/all_to_all | solution.py:125
  135.6 1.6 copy.76
  137.2 2.5 reshape.237
  139.8 10.1 %multiply_add_fusion.1 = (f32[3,256,512]{2,1,0:T(8,128)S(1)}, f32[3,256,512]{2,1,0:T(8,128)}) fusion(f32[3,256,512]{2,1,0:T(8,128)S(1)} %copy-done, f32[3,256,512]{2,1,0:T(8,128)} %param.14, f32[3,256,512]{2,1,0:T(8,128)} %reshape.237, f32[3,258,514]{2,1,0:T(8,128)} %fusion.14, f32[256,512]{1,0:T(8,128)} %get-tuple-element.182, f32[3,260,514]{2,1,0:T(8,128)} %copy-done.4, ...), kind=kLoop, calls=%fused_computation.89 | loop fusion | flops 11010048 | bytes 21520384 | tf_op jit(solution)/shard_map/add | solution.py:138
  149.9 1.7 collective-permute-start.5
  153.0 2.4 copy.77
  155.4 2.4 gather_fusion.3
  158.4 3.3 %collective-permute-start.7 = (f32[3,260,2]{2,1,0:T(8,128)S(1)}, f32[3,260,2]{2,1,0:T(8,128)S(1)}, u32[]{:S(2)}, u32[]{:S(2)}) collective-permute-start(f32[3,260,2]{2,1,0:T(8,128)S(1)} %get-tuple-element.168), channel_id=1, source_target_pairs={{0,1},{1,2},{2,3},{3,4},{4,5},{5,6},{6,7},{8,9},{9,10},{10,11},{11... | collective-permute-start | bytes 18728 | tf_op jit(solution)/shard_map/ppermute | solution.py:27
  164.1 7.3 %all-to-all-start.2 = ((f32[3,128,128]{2,0,1:T(4,128)}), f32[3,128,128]{2,0,1:T(4,128)S(1)}, u32[]{:S(2)}, u32[]{:S(2)}) async-start(f32[3,128,128]{2,0,1:T(4,128)} %bitcast_multiply_fusion), calls=%async_computation.2 | async-start | bytes 524288 | tf_op jit(solution)/shard_map/all_to_all | solution.py:116
  171.4 10.6 %collective-permute-done.7 = f32[3,260,2]{2,1,0:T(8,128)S(1)} collective-permute-done((f32[3,260,2]{2,1,0:T(8,128)S(1)}, f32[3,260,2]{2,1,0:T(8,128)S(1)}, u32[]{:S(2)}, u32[]{:S(2)}) %collective-permute-start.7) | collective-permute-done | bytes 6272 | tf_op jit(solution)/shard_map/ppermute | solution.py:27
  182.0 1.7 pad_maximum_fusion.2
  183.8 1.4 multiply_reduce_fusion.3
  188.3 2.1 pad_maximum_fusion.3
  195.2 63.0 %while.25 = (s32[]{:T(128)}, f32[8,3,32,128]{3,2,0,1:T(8,128)S(1)}, f32[8,3,32,128]{3,2,0,1:T(8,128)S(1)}, f32[8,3,32,128]{3,2,0,1:T(8,128)}, f32[8,3,32,128]{3,2,0,1:T(8,128)S(1)}, /*index=5*/f32[8,32]{1,0:T(8,128)}, s32[]{:T(128)}) while((s32[]{:T(128)}, f32[8,3,32,128]{3,2,0,1:T(8,128)S(1)}, f32[8,3,32,128]{3,2,0,1:T(8,128)S(1)}, ...), condition=%wide.region_17.20_spmd, body=%wide.region_13.19_spmd.sunk | while | flops 11522082 | bytes 9077221 | solution.py:89
  196.7 2.1 fusion.95
  199.1 3.9 %fusion.97 = (f32[3,32,128]{2,1,0:T(8,128)S(1)}, f32[3,32,128]{2,1,0:T(8,128)S(1)}) fusion(f32[32,128,128]{2,1,0:T(8,128)S(1)} %exponential_multiply_fusion.5, f32[3,32,128]{2,1,0:T(8,128)S(1)} %dynamic-slice_bitcast_fusion.10, f32[3,32,128]{2,1,0:T(8,128)S(1)} %dynamic-slice_bitcast_fusion.11), kind=kLoop, calls=%fused_computation.21.clone.1 | loop fusion | flops 6266880 | bytes 2293760 | tf_op jit(solution)/shard_map/while/body/eval_jaxpr/reduce_sum | solution.py:69
  204.5 2.1 fusion.95
  206.9 3.9 %fusion.97 = (f32[3,32,128]{2,1,0:T(8,128)S(1)}, f32[3,32,128]{2,1,0:T(8,128)S(1)}) fusion(f32[32,128,128]{2,1,0:T(8,128)S(1)} %exponential_multiply_fusion.5, f32[3,32,128]{2,1,0:T(8,128)S(1)} %dynamic-slice_bitcast_fusion.10, f32[3,32,128]{2,1,0:T(8,128)S(1)} %dynamic-slice_bitcast_fusion.11), kind=kLoop, calls=%fused_computation.21.clone.1 | loop fusion | flops 6266880 | bytes 2293760 | tf_op jit(solution)/shard_map/while/body/eval_jaxpr/reduce_sum | solution.py:69
  212.4 2.1 fusion.95
  214.8 3.9 %fusion.97 = (f32[3,32,128]{2,1,0:T(8,128)S(1)}, f32[3,32,128]{2,1,0:T(8,128)S(1)}) fusion(f32[32,128,128]{2,1,0:T(8,128)S(1)} %exponential_multiply_fusion.5, f32[3,32,128]{2,1,0:T(8,128)S(1)} %dynamic-slice_bitcast_fusion.10, f32[3,32,128]{2,1,0:T(8,128)S(1)} %dynamic-slice_bitcast_fusion.11), kind=kLoop, calls=%fused_computation.21.clone.1 | loop fusion | flops 6266880 | bytes 2293760 | tf_op jit(solution)/shard_map/while/body/eval_jaxpr/reduce_sum | solution.py:69
  220.3 2.1 fusion.95
  222.7 3.9 %fusion.97 = (f32[3,32,128]{2,1,0:T(8,128)S(1)}, f32[3,32,128]{2,1,0:T(8,128)S(1)}) fusion(f32[32,128,128]{2,1,0:T(8,128)S(1)} %exponential_multiply_fusion.5, f32[3,32,128]{2,1,0:T(8,128)S(1)} %dynamic-slice_bitcast_fusion.10, f32[3,32,128]{2,1,0:T(8,128)S(1)} %dynamic-slice_bitcast_fusion.11), kind=kLoop, calls=%fused_computation.21.clone.1 | loop fusion | flops 6266880 | bytes 2293760 | tf_op jit(solution)/shard_map/while/body/eval_jaxpr/reduce_sum | solution.py:69
  228.2 2.1 fusion.95
  230.5 3.9 %fusion.97 = (f32[3,32,128]{2,1,0:T(8,128)S(1)}, f32[3,32,128]{2,1,0:T(8,128)S(1)}) fusion(f32[32,128,128]{2,1,0:T(8,128)S(1)} %exponential_multiply_fusion.5, f32[3,32,128]{2,1,0:T(8,128)S(1)} %dynamic-slice_bitcast_fusion.10, f32[3,32,128]{2,1,0:T(8,128)S(1)} %dynamic-slice_bitcast_fusion.11), kind=kLoop, calls=%fused_computation.21.clone.1 | loop fusion | flops 6266880 | bytes 2293760 | tf_op jit(solution)/shard_map/while/body/eval_jaxpr/reduce_sum | solution.py:69
  236.0 2.1 fusion.95
  238.4 3.9 %fusion.97 = (f32[3,32,128]{2,1,0:T(8,128)S(1)}, f32[3,32,128]{2,1,0:T(8,128)S(1)}) fusion(f32[32,128,128]{2,1,0:T(8,128)S(1)} %exponential_multiply_fusion.5, f32[3,32,128]{2,1,0:T(8,128)S(1)} %dynamic-slice_bitcast_fusion.10, f32[3,32,128]{2,1,0:T(8,128)S(1)} %dynamic-slice_bitcast_fusion.11), kind=kLoop, calls=%fused_computation.21.clone.1 | loop fusion | flops 6266880 | bytes 2293760 | tf_op jit(solution)/shard_map/while/body/eval_jaxpr/reduce_sum | solution.py:69
  243.9 2.1 fusion.95
  246.3 3.9 %fusion.97 = (f32[3,32,128]{2,1,0:T(8,128)S(1)}, f32[3,32,128]{2,1,0:T(8,128)S(1)}) fusion(f32[32,128,128]{2,1,0:T(8,128)S(1)} %exponential_multiply_fusion.5, f32[3,32,128]{2,1,0:T(8,128)S(1)} %dynamic-slice_bitcast_fusion.10, f32[3,32,128]{2,1,0:T(8,128)S(1)} %dynamic-slice_bitcast_fusion.11), kind=kLoop, calls=%fused_computation.21.clone.1 | loop fusion | flops 6266880 | bytes 2293760 | tf_op jit(solution)/shard_map/while/body/eval_jaxpr/reduce_sum | solution.py:69
  251.8 2.1 fusion.95
  254.2 3.9 %fusion.97 = (f32[3,32,128]{2,1,0:T(8,128)S(1)}, f32[3,32,128]{2,1,0:T(8,128)S(1)}) fusion(f32[32,128,128]{2,1,0:T(8,128)S(1)} %exponential_multiply_fusion.5, f32[3,32,128]{2,1,0:T(8,128)S(1)} %dynamic-slice_bitcast_fusion.10, f32[3,32,128]{2,1,0:T(8,128)S(1)} %dynamic-slice_bitcast_fusion.11), kind=kLoop, calls=%fused_computation.21.clone.1 | loop fusion | flops 6266880 | bytes 2293760 | tf_op jit(solution)/shard_map/while/body/eval_jaxpr/reduce_sum | solution.py:69
  260.8 5.3 %all-to-all-start.3 = ((f32[3,128,128]{2,0,1:T(4,128)}), f32[3,128,128]{2,0,1:T(4,128)S(1)}, u32[]{:S(2)}, u32[]{:S(2)}) async-start(f32[3,128,128]{2,0,1:T(4,128)} %copy.86), calls=%async_computation.3 | async-start | bytes 524288 | tf_op jit(solution)/shard_map/all_to_all | solution.py:125
  266.2 7.1 %fusion.11 = f32[3,258,514]{2,1,0:T(8,128)} fusion(f32[3,260,516]{2,1,0:T(8,128)} %pad_maximum_fusion.3, f32[3,260,514]{2,1,0:T(8,128)} %copy-done.2, f32[3,260,514]{2,1,0:T(8,128)} %copy-done.1, f32[258,514]{1,0:T(8,128)S(1)} %copy-done.7), kind=kLoop, calls=%fused_computation.34 | loop fusion | flops 2387016 | bytes 10078512 | tf_op jit(solution)/shard_map/mul | solution.py:107
  273.3 3.3 %all-to-all-done.3 = f32[3,128,128]{2,0,1:T(4,128)S(1)} async-done(((f32[3,128,128]{2,0,1:T(4,128)}), f32[3,128,128]{2,0,1:T(4,128)S(1)}, u32[]{:S(2)}, u32[]{:S(2)}) %all-to-all-start.3) | async-done | bytes 196640 | tf_op jit(solution)/shard_map/all_to_all | solution.py:125
  277.4 1.6 copy.88
  279.0 2.7 reshape.243
  281.8 10.1 %multiply_add_fusion = (f32[3,256,512]{2,1,0:T(8,128)}, f32[3,256,512]{2,1,0:T(8,128)}) fusion(f32[3,256,512]{2,1,0:T(8,128)S(1)} %get-tuple-element.160, f32[3,256,512]{2,1,0:T(8,128)S(1)} %copy-done.5, f32[3,256,512]{2,1,0:T(8,128)} %reshape.243, f32[3,258,514]{2,1,0:T(8,128)} %fusion.11, f32[256,512]{1,0:T(8,128)} %multiply_add_fusion.2, ...), kind=kLoop, calls=%fused_computation.84 | loop fusion | flops 11010048 | bytes 21520384 | tf_op jit(solution)/shard_map/add | solution.py:138
  (214 shorter events, 57.3 us)
Async XLA Ops:
  1.5 22.0 %collective-permute-start.1 = (f32[3,2,512]{2,1,0:T(2,128)S(1)}, f32[3,2,512]{2,1,0:T(2,128)S(1)}, u32[]{:S(2)}, u32[]{:S(2)}) collective-permute-start(f32[3,2,512]{2,1,0:T(2,128)S(1)} %get-tuple-element.176), channel_id=1, source_target_pairs={{0,8},{8,16},{16,24},{1,9},{9,17},{17,25},{2,10},{10,18},{18,26},{... | collective-permute-start | bytes 36872 | tf_op jit(solution)/shard_map/ppermute | solution.py:27
  3.8 19.6 %collective-permute-start = (f32[3,2,512]{2,1,0:T(2,128)S(1)}, f32[3,2,512]{2,1,0:T(2,128)S(1)}, u32[]{:S(2)}, u32[]{:S(2)}) collective-permute-start(f32[3,2,512]{2,1,0:T(2,128)S(1)} %get-tuple-element.177), channel_id=1, source_target_pairs={{8,0},{16,8},{24,16},{9,1},{17,9},{25,17},{10,2},{18,10},{26,18},{... | collective-permute-start | bytes 36872 | tf_op jit(solution)/shard_map/ppermute | solution.py:29
  6.5 6.4 %copy-start.28 = (pred[128]{0:T(512)(128)(4,1)}, pred[128]{0:T(512)(128)(4,1)S(1)}, u32[]{:S(2)}) copy-start(pred[128]{0:T(512)(128)(4,1)S(1)} %get-tuple-element.180) | copy-start | bytes 388
  6.5 6.4 %copy-start.30 = (f32[128]{0:T(128)}, f32[128]{0:T(128)S(1)}, u32[]{:S(2)}) copy-start(f32[128]{0:T(128)S(1)} %get-tuple-element.181) | copy-start | bytes 1540
  7.9 15.2 %copy-start.22 = (s32[1,1,2,256]{3,2,1,0:T(2,128)S(1)}, s32[1,1,2,256]{3,2,1,0:T(2,128)}, u32[]{:S(2)}) copy-start(s32[1,1,2,256]{3,2,1,0:T(2,128)} %param.17) | copy-start | bytes 6148
  10.3 13.1 %copy-start = (f32[3,256,512]{2,1,0:T(8,128)S(1)}, f32[3,256,512]{2,1,0:T(8,128)}, u32[]{:S(2)}) copy-start(f32[3,256,512]{2,1,0:T(8,128)} %param.13) | copy-start | bytes 4718596
  13.9 40.0 %all-to-all-start = ((f32[3,128,128]{2,0,1:T(4,128)}), f32[3,128,128]{2,0,1:T(4,128)S(1)}, u32[]{:S(2)}, u32[]{:S(2)}) async-start(f32[3,128,128]{2,0,1:T(4,128)} %bitcast_multiply_fusion.1), calls=%async_computation | async-start | bytes 524288 | tf_op jit(solution)/shard_map/all_to_all | solution.py:116
  23.1 92.2 %copy-start.18 = (s32[1,1,1,256]{3,2,1,0:T(1,128)}, s32[1,1,1,256]{3,2,1,0:T(1,128)S(1)}, u32[]{:S(2)}) copy-start(s32[1,1,1,256]{3,2,1,0:T(1,128)S(1)} %get-tuple-element.179) | copy-start | bytes 3076
  23.2 93.1 %copy-start.16 = (s32[1,1,1,256]{3,2,1,0:T(1,128)}, s32[1,1,1,256]{3,2,1,0:T(1,128)S(1)}, u32[]{:S(2)}) copy-start(s32[1,1,1,256]{3,2,1,0:T(1,128)S(1)} %get-tuple-element.178) | copy-start | bytes 3076
  23.2 33.1 %copy-start.24 = (pred[256]{0:T(512)(128)(4,1)}, pred[256]{0:T(512)(128)(4,1)S(1)}, u32[]{:S(2)}) copy-start(pred[256]{0:T(512)(128)(4,1)S(1)} %compare_and_fusion.1) | copy-start | bytes 772
  23.2 31.7 %copy-start.26 = (pred[256]{0:T(512)(128)(4,1)}, pred[256]{0:T(512)(128)(4,1)S(1)}, u32[]{:S(2)}) copy-start(pred[256]{0:T(512)(128)(4,1)S(1)} %compare_and_fusion) | copy-start | bytes 772
  23.4 100.8 %copy-start.6 = (f32[258,514]{1,0:T(8,128)}, f32[258,514]{1,0:T(8,128)S(1)}, u32[]{:S(2)}) copy-start(f32[258,514]{1,0:T(8,128)S(1)} %and_convert_fusion) | copy-start | bytes 1591348
  23.4 30.5 %copy-start.20 = (s32[1024]{0:T(1024)}, s32[1024]{0:T(1024)S(1)}, u32[]{:S(2)}) copy-start(s32[1024]{0:T(1024)S(1)} %pad_clamp_fusion) | copy-start | bytes 12292
  24.6 22.3 %collective-permute-start.3 = (f32[3,260,2]{2,1,0:T(8,128)}, f32[3,260,2]{2,1,0:T(8,128)S(1)}, u32[]{:S(2)}, u32[]{:S(2)}) collective-permute-start(f32[3,260,2]{2,1,0:T(8,128)} %get-tuple-element.172), channel_id=1, source_target_pairs={{0,1},{1,2},{2,3},{3,4},{4,5},{5,6},{6,7},{8,9},{9,10},{10,11},{11... | collective-permute-start | bytes 18728 | tf_op jit(solution)/shard_map/ppermute | solution.py:27
  28.3 18.6 %collective-permute-start.2 = (f32[3,260,2]{2,1,0:T(8,128)}, f32[3,260,2]{2,1,0:T(8,128)S(1)}, u32[]{:S(2)}, u32[]{:S(2)}) collective-permute-start(f32[3,260,2]{2,1,0:T(8,128)} %get-tuple-element.173), channel_id=1, source_target_pairs={{1,0},{2,1},{3,2},{4,3},{5,4},{6,5},{7,6},{9,8},{10,9},{11,10},{12... | collective-permute-start | bytes 18728 | tf_op jit(solution)/shard_map/ppermute | solution.py:29
  29.6 25.7 %copy-start.21 = (s32[1024]{0:T(1024)}, s32[1024]{0:T(1024)S(1)}, u32[]{:S(2)}) copy-start(s32[1024]{0:T(1024)S(1)} %pad_clamp_fusion.1) | copy-start | bytes 12292
  47.7 1.4 copy-start.3
  47.7 1.9 copy-start.4
  115.3 16.0 %copy-start.23 = (f32[8,32]{1,0:T(8,128)}, f32[8,32]{1,0:T(8,128)S(1)}, u32[]{:S(2)}) copy-start(f32[8,32]{1,0:T(8,128)S(1)} %get-tuple-element.336) | copy-start | bytes 3076
  118.0 16.7 %all-to-all-start.1 = ((f32[3,128,128]{2,0,1:T(4,128)}), f32[3,128,128]{2,0,1:T(4,128)S(1)}, u32[]{:S(2)}, u32[]{:S(2)}) async-start(f32[3,128,128]{2,0,1:T(4,128)} %copy.74), calls=%async_computation.1 | async-start | bytes 524288 | tf_op jit(solution)/shard_map/all_to_all | solution.py:125
  124.2 10.5 %copy-start.32 = (s32[1,1,128]{2,1,0:T(1,128)S(1)}, s32[1,1,128]{2,1,0:T(1,128)}, u32[]{:S(2)}) copy-start(s32[1,1,128]{2,1,0:T(1,128)} %param.16) | copy-start | bytes 1540
  149.9 7.9 %collective-permute-start.5 = (f32[3,2,512]{2,1,0:T(2,128)S(1)}, f32[3,2,512]{2,1,0:T(2,128)S(1)}, u32[]{:S(2)}, u32[]{:S(2)}) collective-permute-start(f32[3,2,512]{2,1,0:T(2,128)S(1)} %get-tuple-element.174), channel_id=1, source_target_pairs={{0,8},{8,16},{16,24},{1,9},{9,17},{17,25},{2,10},{10,18},{18,26},{... | collective-permute-start | bytes 36872 | tf_op jit(solution)/shard_map/ppermute | solution.py:27
  151.6 6.2 %collective-permute-start.4 = (f32[3,2,512]{2,1,0:T(2,128)S(1)}, f32[3,2,512]{2,1,0:T(2,128)S(1)}, u32[]{:S(2)}, u32[]{:S(2)}) collective-permute-start(f32[3,2,512]{2,1,0:T(2,128)S(1)} %get-tuple-element.175), channel_id=1, source_target_pairs={{8,0},{16,8},{24,16},{9,1},{17,9},{25,17},{10,2},{18,10},{26,18},{... | collective-permute-start | bytes 36872 | tf_op jit(solution)/shard_map/ppermute | solution.py:29
  155.4 7.6 %copy-start.29 = (pred[128]{0:T(512)(128)(4,1)S(1)}, pred[128]{0:T(512)(128)(4,1)}, u32[]{:S(2)}) copy-start(pred[128]{0:T(512)(128)(4,1)} %copy-done.28) | copy-start | bytes 388
  155.4 7.6 %copy-start.31 = (f32[128]{0:T(128)S(1)}, f32[128]{0:T(128)}, u32[]{:S(2)}) copy-start(f32[128]{0:T(128)} %copy-done.30) | copy-start | bytes 1540
  157.8 0.6 copy-start.10
  157.8 0.6 copy-start.13
  158.4 23.6 %collective-permute-start.7 = (f32[3,260,2]{2,1,0:T(8,128)S(1)}, f32[3,260,2]{2,1,0:T(8,128)S(1)}, u32[]{:S(2)}, u32[]{:S(2)}) collective-permute-start(f32[3,260,2]{2,1,0:T(8,128)S(1)} %get-tuple-element.168), channel_id=1, source_target_pairs={{0,1},{1,2},{2,3},{3,4},{4,5},{5,6},{6,7},{8,9},{9,10},{10,11},{11... | collective-permute-start | bytes 18728 | tf_op jit(solution)/shard_map/ppermute | solution.py:27
  161.7 20.3 %collective-permute-start.6 = (f32[3,260,2]{2,1,0:T(8,128)S(1)}, f32[3,260,2]{2,1,0:T(8,128)S(1)}, u32[]{:S(2)}, u32[]{:S(2)}) collective-permute-start(f32[3,260,2]{2,1,0:T(8,128)S(1)} %get-tuple-element.169), channel_id=1, source_target_pairs={{1,0},{2,1},{3,2},{4,3},{5,4},{6,5},{7,6},{9,8},{10,9},{11,10},{12... | collective-permute-start | bytes 18728 | tf_op jit(solution)/shard_map/ppermute | solution.py:29
  164.1 27.2 %all-to-all-start.2 = ((f32[3,128,128]{2,0,1:T(4,128)}), f32[3,128,128]{2,0,1:T(4,128)S(1)}, u32[]{:S(2)}, u32[]{:S(2)}) async-start(f32[3,128,128]{2,0,1:T(4,128)} %bitcast_multiply_fusion), calls=%async_computation.2 | async-start | bytes 524288 | tf_op jit(solution)/shard_map/all_to_all | solution.py:116
  171.4 12.3 %copy-start.11 = (f32[3,2,512]{2,1,0:T(2,128)S(1)}, f32[3,2,512]{2,1,0:T(2,128)}, u32[]{:S(2)}) copy-start(f32[3,2,512]{2,1,0:T(2,128)} %copy-done.10) | copy-start | bytes 36868
  171.4 12.3 %copy-start.14 = (f32[3,2,512]{2,1,0:T(2,128)S(1)}, f32[3,2,512]{2,1,0:T(2,128)}, u32[]{:S(2)}) copy-start(f32[3,2,512]{2,1,0:T(2,128)} %copy-done.13) | copy-start | bytes 36868
  182.0 1.7 copy-start.8
  183.7 1.4 copy-start.1
  183.7 1.9 copy-start.2
  185.7 2.6 copy-start.9
  190.4 2.0 copy-start.27
  192.4 1.5 copy-start.25
  195.1 63.0 %copy-start.19 = (s32[1,1,1,256]{3,2,1,0:T(1,128)S(1)}, s32[1,1,1,256]{3,2,1,0:T(1,128)}, u32[]{:S(2)}) copy-start(s32[1,1,1,256]{3,2,1,0:T(1,128)} %copy-done.18) | copy-start | bytes 3076
  195.2 63.9 %copy-start.17 = (s32[1,1,1,256]{3,2,1,0:T(1,128)S(1)}, s32[1,1,1,256]{3,2,1,0:T(1,128)}, u32[]{:S(2)}) copy-start(s32[1,1,1,256]{3,2,1,0:T(1,128)} %copy-done.16) | copy-start | bytes 3076
  258.1 8.0 %copy-start.7 = (f32[258,514]{1,0:T(8,128)S(1)}, f32[258,514]{1,0:T(8,128)}, u32[]{:S(2)}) copy-start(f32[258,514]{1,0:T(8,128)} %copy-done.6) | copy-start | bytes 1591348
  260.8 15.7 %all-to-all-start.3 = ((f32[3,128,128]{2,0,1:T(4,128)}), f32[3,128,128]{2,0,1:T(4,128)S(1)}, u32[]{:S(2)}, u32[]{:S(2)}) async-start(f32[3,128,128]{2,0,1:T(4,128)} %copy.86), calls=%async_computation.3 | async-start | bytes 524288 | tf_op jit(solution)/shard_map/all_to_all | solution.py:125
  266.2 10.4 %copy-start.33 = (s32[1,1,128]{2,1,0:T(1,128)S(1)}, s32[1,1,128]{2,1,0:T(1,128)}, u32[]{:S(2)}) copy-start(s32[1,1,128]{2,1,0:T(1,128)} %param.16) | copy-start | bytes 1540
  279.0 2.7 copy-start.5
  279.0 2.7 copy-start.12
  279.0 2.7 copy-start.15
where the time goes:
time: 294 us; the launch traced here: 292 us
  other arithmetic  163 us (55%)
  starting transfers between devices  44.3 us (15%)
  local copies, waits for them, and re-layouts  42.9 us (15%)
  waiting for transfers between devices  34.4 us (12%)
  matrix products  5.33 us (2%)
    reduce_sum x16, other arithmetic, pair_block(): return (jnp.sum(push, axis=3), -jnp.sum(push, axis=2))  63.1 us
    reduce_sum x16, other arithmetic, pair_block(): jnp.sum(offset * offset, axis=0)  33 us
    ppermute x4, waiting for transfers between devices, extended(): lax.ppermute(tail, axis, [(i, (i + 1) % count) for i in range(ends)])  27.8 us
    add x2, other arithmetic, local(): positions = positions + time_step * velocity  20.2 us
    all_to_all x2, starting transfers between devices, contact_force(): lax.all_to_all(sent, ('gx', 'gy'), split_axis=1, concat_axis=1, tiled=True)  16.5 us
    mul x2, other arithmetic, internal(): curve = laplace(wide) * inside[None]  14.2 us
    sub x32, local copies, waits for them, and re-layouts, pair_block(): offset = near[:, :, :, None] - far[:, :, None, :]  13.1 us
    all_to_all x2, starting transfers between devices, contact_force(): lax.all_to_all(slot_force, ('gx', 'gy'), split_axis=1, concat_axis=1, til...  11.6 us
  transfers between devices with their start and end apart: 12, of which 4 were waited for; matrix products, arithmetic and copies ran while one was open for 16% of the time, Pallas kernels for 0%

commit v1 on v0

v1 whole, which is shorter than its diff:
```python
import functools
import math

import jax
import jax.numpy as jnp
from jax import lax
from jax.experimental import pallas as pl
from jax.experimental.pallas import tpu as pltpu
from jax.sharding import PartitionSpec as P

TILE = 128
STEPS = 2
MESH = pl.DeviceIdType.MESH

time_step = 0.1
damping = 0.2
hardening = 0.1
bend_gain = 0.02
SCALE = math.sqrt(0.5 * math.log2(math.e))
CHUNK = 32
UNROLL = 4
bf16 = jnp.bfloat16
f32 = jnp.float32


def split3(x):
    hi = x.astype(bf16)
    rest = x - hi.astype(f32)
    mid = rest.astype(bf16)
    lo = (rest - mid.astype(f32)).astype(bf16)
    return hi, mid, lo


def kernel(ngx, ngy, slots, pos_ref, vel_ref, stiff_ref, route_s, route_v, pair_s, pair_v,
           pos_out, vel_out, xpad, blocks, force, sendbuf, recv, backsend, back, rec8, aug, pairsum,
           colsend, colrecv, rowrecv, cornrecv,
           tile_send, tile_recv, back_send, back_recv, halo_send, halo_recv):
    n = ngx * ngy
    rows, cols = pos_ref.shape[1], pos_ref.shape[2]
    wide = cols + TILE
    number = pair_s.shape[1]
    total = n * slots
    gi = lax.axis_index("gx")
    gj = lax.axis_index("gy")
    me = gi * ngy + gj

    def place(o):
        return (o // ngy, lax.rem(o, ngy))

    barrier = pltpu.get_barrier_semaphore()

    def greet(d, carry):
        pl.semaphore_signal(barrier, inc=1, device_id=place(lax.rem(me + d, n)), device_id_type=MESH)
        return carry

    lax.fori_loop(1, n, greet, 0)

    for c in range(3):
        xpad[c, 8:8 + rows, 0:cols] = pos_ref[c]
        for t in range(cols // TILE):
            blocks[t, c] = pos_ref[c, :, t * TILE:(t + 1) * TILE]
    vel_out[...] = vel_ref[...]
    rec8[...] = jnp.zeros_like(rec8)
    rec8[:, 3, :] = jnp.ones((total, TILE), f32)

    pl.semaphore_wait(barrier, n - 1)

    up = lax.rem(gi + ngx - 1, ngx)
    down = lax.rem(gi + 1, ngx)
    left = lax.rem(gj + ngy - 1, ngy)
    right = lax.rem(gj + 1, ngy)
    has_up = (gi > 0).astype(f32)
    has_down = (gi < ngx - 1).astype(f32)
    has_left = (gj > 0).astype(f32)
    has_right = (gj < ngy - 1).astype(f32)

    def tile_copy(step, o, source):
        return pltpu.make_async_remote_copy(
            src_ref=sendbuf.at[step, o], dst_ref=recv.at[step, source],
            send_sem=tile_send.at[step, o], recv_sem=tile_recv.at[step, source],
            device_id=place(o), device_id_type=MESH)

    def back_copy(step, o, source):
        return pltpu.make_async_remote_copy(
            src_ref=backsend.at[step, o], dst_ref=back.at[step, source],
            send_sem=back_send.at[step, o], recv_sem=back_recv.at[step, source],
            device_id=place(o), device_id_type=MESH)

    def run_step(step, carry):
        def fetch(o, put):
            for k in range(slots):
                at = k * n + o
                row = route_s[0, at]
                col = route_s[1, at]
                filled = (row >= 0).astype(f32)
                row = jnp.maximum(row, 0)
                col = jnp.maximum(col, 0)
                for c in range(3):
                    put(k * 3 + c, blocks[col, c, pl.ds(row, 1), :] * filled)

        def send_tiles(d, carry):
            o = lax.rem(me + d, n)

            def put(j, value):
                sendbuf[step, o, pl.ds(j, 1), :] = value

            fetch(o, put)
            tile_copy(step, o, me).start()
            return carry

        lax.fori_loop(1, n, send_tiles, 0)

        def put_own(j, value):
            recv[step, me, pl.ds(j, 1), :] = value

        fetch(me, put_own)

        lane = lax.broadcasted_iota(jnp.int32, (rows, TILE), 1)
        packed = jnp.zeros((rows, TILE), f32)
        for c in range(3):
            first = pltpu.roll(xpad[c, 8:8 + rows, 0:TILE], 2 * c, 1) if c else xpad[c, 8:8 + rows, 0:TILE]
            last = pltpu.roll(xpad[c, 8:8 + rows, cols - TILE:cols], 10 + 2 * c, 1)
            packed = jnp.where((lane == 2 * c) | (lane == 2 * c + 1), first, packed)
            packed = jnp.where((lane == 8 + 2 * c) | (lane == 9 + 2 * c), last, packed)
        turned = jnp.transpose(packed)
        colsend[step, 0] = turned[0:8]
        colsend[step, 1] = turned[8:16]

        top = pl.ds(8, 8)
        bottom = pl.ds(rows, 8)
        head = pl.ds(0, TILE)
        tail = pl.ds(cols - TILE, TILE)
        plans = (
            (colsend.at[step, 0], colrecv.at[step, 1], (gi, left)),
            (colsend.at[step, 1], colrecv.at[step, 0], (gi, right)),
            (xpad.at[:, top, pl.ds(0, cols)], rowrecv.at[step, 1], (up, gj)),
            (xpad.at[:, bottom, pl.ds(0, cols)], rowrecv.at[step, 0], (down, gj)),
            (xpad.at[:, bottom, tail], cornrecv.at[step, 0], (down, right)),
            (xpad.at[:, bottom, head], cornrecv.at[step, 1], (down, left)),
            (xpad.at[:, top, tail], cornrecv.at[step, 2], (up, right)),
            (xpad.at[:, top, head], cornrecv.at[step, 3], (up, left)),
        )
        halos = [
            pltpu.make_async_remote_copy(
                src_ref=src, dst_ref=dst, send_sem=halo_send.at[step, i], recv_sem=halo_recv.at[step, i],
                device_id=where, device_id_type=MESH)
            for i, (src, dst, where) in enumerate(plans)
        ]
        for copy in halos:
            copy.start()
        for copy in halos:
            copy.wait()

        joined = jnp.concatenate(
            [colrecv[step, 0], colrecv[step, 1], jnp.zeros((TILE - 16, rows), f32)], axis=0)
        sides = jnp.transpose(joined)
        lane8 = lax.broadcasted_iota(jnp.int32, (8, TILE), 1)
        for c in range(3):
            before = pltpu.roll(sides, 126 - 2 * c, 1) * has_left
            after = pltpu.roll(sides, 120 - 2 * c, 1) * has_right
            xpad[c, 8:8 + rows, cols:wide] = jnp.where(lane < 64, after, before)
            xpad[c, 0:8, 0:cols] = rowrecv[step, 0, c] * has_up
            xpad[c, 8 + rows:16 + rows, 0:cols] = rowrecv[step, 1, c] * has_down
            xpad[c, 0:8, cols:wide] = jnp.where(
                lane8 < 64, cornrecv[step, 1, c] * has_right, cornrecv[step, 0, c] * has_left) * has_up
            xpad[c, 8 + rows:16 + rows, cols:wide] = jnp.where(
                lane8 < 64, cornrecv[step, 3, c] * has_right, cornrecv[step, 2, c] * has_left) * has_down

        tall = CHUNK + 16

        def above(v):
            return pltpu.roll(v, 1, 0)

        def below(v):
            return pltpu.roll(v, tall - 1, 0)

        def before(v):
            return pltpu.roll(v, 1, 1)

        def after(v):
            return pltpu.roll(v, wide - 1, 1)

        def internal(chunk, carry):
            r0 = pl.multiple_of(chunk * CHUNK, CHUNK)
            x = [xpad[c, pl.ds(r0, tall), :] for c in range(3)]
            xa = [after(v) for v in x]
            xb = [below(v) for v in x]
            row = lax.broadcasted_iota(jnp.int32, (tall, wide), 0) + (r0 - 8)
            col = lax.broadcasted_iota(jnp.int32, (tall, wide), 1)
            mask = jnp.where(row < 0, has_up, jnp.where(row >= rows, has_down, 1.0))
            mask = mask * jnp.where(col == cols, has_right, jnp.where(col == wide - 1, has_left, 1.0))
            ea = [p - q for p, q in zip(xa, x)]
            eb = [p - q for p, q in zip(xb, x)]
            ga = 1.0 + hardening * (ea[0] * ea[0] + ea[1] * ea[1] + ea[2] * ea[2])
            gb = 1.0 + hardening * (eb[0] * eb[0] + eb[1] * eb[1] + eb[2] * eb[2])
            stiff = stiff_ref[pl.ds(r0, CHUNK), :]
            for c in range(3):
                fa = ea[c] * ga
                fb = eb[c] * gb
                pull = (fa - before(fa)) + (fb - above(fb))
                curve = ((ea[c] - before(ea[c])) + (eb[c] - above(eb[c]))) * mask
                bend = (above(curve) + below(curve)) + (before(curve) + after(curve)) - 4.0 * curve
                force[c, pl.ds(r0, CHUNK), :] = (
                    stiff * pull[8:8 + CHUNK, 0:cols] - bend_gain * bend[8:8 + CHUNK, 0:cols])
            return carry

        lax.fori_loop(0, rows // CHUNK, internal, 0)

        def tiles_in(d, carry):
            tile_copy(step, me, lax.rem(me + d, n)).wait_recv()
            return carry

        lax.fori_loop(1, n, tiles_in, 0)
        for k in range(slots):
            for c in range(3):
                rec8[k * n:(k + 1) * n, c, :] = recv[step, :, k * 3 + c, :] * SCALE

        def split_slots(g, carry):
            at = pl.ds(g * 8, 8)
            hi, mid, lo = split3(rec8[at])
            second = mid.astype(f32) + pltpu.roll(lo.astype(f32), 4, 1)
            aug[at] = jnp.concatenate([hi.astype(f32), second], axis=1).astype(bf16)
            return carry

        lax.fori_loop(0, total // 8, split_slots, 0)

        def sums(out):
            out = out[0:8] + out[8:16]
            return out + pltpu.roll(out, 4, 0)

        def pairs(g, carry):
            for u in range(UNROLL):
                m = g * UNROLL + u
                a = jnp.maximum(pair_s[0, m], 0)
                b = jnp.maximum(pair_s[1, m], 0)
                p = jnp.transpose(rec8[a])
                q = rec8[b]
                power = jnp.full((TILE, TILE), -2.0, f32)
                for c in range(3):
                    d = p[:, c:c + 1] - q[c:c + 1, :]
                    power = power - d * d
                w = jnp.exp2(power)
                hi = w.astype(bf16)
                lo = (w - hi.astype(f32)).astype(bf16)
                pa = aug[a]
                qb = aug[b]
                pa = jnp.concatenate([pa, pa], axis=1)
                qb = jnp.concatenate([qb, qb], axis=1)
                far = jnp.dot(pa, jnp.concatenate([hi, lo], axis=0), preferred_element_type=f32)
                near = lax.dot_general(
                    qb, jnp.concatenate([hi, lo], axis=1), (((1,), (1,)), ((), ())),
                    preferred_element_type=f32)
                pairsum[m] = sums(near)
                pairsum[number + m] = sums(far)
            return carry

        lax.fori_loop(0, number // UNROLL, pairs, 0)

        ids = lax.broadcasted_iota(jnp.int32, (total, number), 0)
        hot = jnp.concatenate(
            [(ids == pair_v[0:1, :]).astype(f32), (ids == pair_v[1:2, :]).astype(f32)], axis=1).astype(bf16)
        summed = []
        for c in range(4):
            parts = split3(pairsum[:, c, :])
            summed.append(sum(jnp.dot(hot, part, preferred_element_type=f32) for part in parts))
        for c in range(3):
            push = (rec8[:, c, :] * summed[3] - summed[c]) * (1.0 / SCALE)
            for k in range(slots):
                backsend[step, :, k * 3 + c, :] = push[k * n:(k + 1) * n]

        def send_back(d, carry):
            back_copy(step, lax.rem(me + d, n), me).start()
            return carry

        lax.fori_loop(1, n, send_back, 0)
        back[step, me] = backsend[step, me]

        def back_in(d, carry):
            back_copy(step, me, lax.rem(me + d, n)).wait_recv()
            return carry

        lax.fori_loop(1, n, back_in, 0)

        parts = [split3(jnp.concatenate([back[step, :, k * 3 + c, :] for k in range(slots)], axis=0))
                 for c in range(3)]
        parts = [jnp.concatenate([parts[c][i] for c in range(3)], axis=1) for i in range(3)]
        parts = jnp.concatenate(parts, axis=0)

        def advance(chunk, carry):
            r0 = pl.multiple_of(chunk * CHUNK, CHUNK)
            span = pl.ds(r0, CHUNK)
            ids = lax.broadcasted_iota(jnp.int32, (CHUNK, total), 0) + r0
            in_row = ids == route_v[0:1, :]
            for t in range(cols // TILE):
                at = slice(t * TILE, (t + 1) * TILE)
                hot = (in_row & (route_v[1:2, :] == t)).astype(f32).astype(bf16)
                hot = jnp.concatenate([hot, hot, hot], axis=1)
                contact = jnp.dot(hot, parts, preferred_element_type=f32)
                for c in range(3):
                    v = vel_out[c, span, at]
                    push = force[c, span, at] + contact[:, c * TILE:(c + 1) * TILE]
                    v = v + time_step * (push - damping * v)
                    x = xpad[c, pl.ds(r0 + 8, CHUNK), at] + time_step * v
                    vel_out[c, span, at] = v
                    xpad[c, pl.ds(r0 + 8, CHUNK), at] = x
                    blocks[t, c, span, :] = x
                    pos_out[c, span, at] = x
            return carry

        lax.fori_loop(0, rows // CHUNK, advance, 0)

        def sent(d, carry):
            o = lax.rem(me + d, n)
            tile_copy(step, o, me).wait_send()
            back_copy(step, o, me).wait_send()
            return carry

        lax.fori_loop(1, n, sent, 0)
        return carry

    lax.fori_loop(0, STEPS, run_step, 0)


def local(ngx, ngy, positions, velocity, stiffness, send_tiles, pair_tiles):
    n = ngx * ngy
    rows, cols = stiffness.shape
    route = send_tiles.reshape(n, -1).T.reshape(-1)
    slots = route.shape[0] // n
    total = n * slots
    per_row = cols // TILE
    route = jnp.where(route >= 0, jnp.stack([route // per_row, route % per_row]), -1)
    paired = pair_tiles.reshape(2, -1)
    paired = jnp.where(paired >= 0, (paired % slots) * n + paired // slots, -1)
    number = paired.shape[1]
    vmem = pl.BlockSpec(memory_space=pltpu.VMEM)
    smem = pl.BlockSpec(memory_space=pltpu.SMEM)
    dma = pltpu.SemaphoreType.DMA
    shape = jax.ShapeDtypeStruct(positions.shape, f32)
    return pl.pallas_call(
        functools.partial(kernel, ngx, ngy, slots),
        out_shape=(shape, shape),
        in_specs=[vmem, vmem, vmem, smem, vmem, smem, vmem],
        out_specs=(vmem, vmem),
        scratch_shapes=[
            pltpu.VMEM((3, rows + 16, cols + TILE), f32),
            pltpu.VMEM((cols // TILE, 3, rows, TILE), f32),
            pltpu.VMEM((3, rows, cols), f32),
            pltpu.VMEM((STEPS, n, slots * 3, TILE), f32),
            pltpu.VMEM((STEPS, n, slots * 3, TILE), f32),
            pltpu.VMEM((STEPS, n, slots * 3, TILE), f32),
            pltpu.VMEM((STEPS, n, slots * 3, TILE), f32),
            pltpu.VMEM((total, 8, TILE), f32),
            pltpu.VMEM((total, 16, TILE), bf16),
            pltpu.VMEM((2 * number, 8, TILE), f32),
            pltpu.VMEM((STEPS, 2, 8, rows), f32),
            pltpu.VMEM((STEPS, 2, 8, rows), f32),
            pltpu.VMEM((STEPS, 2, 3, 8, cols), f32),
            pltpu.VMEM((STEPS, 4, 3, 8, TILE), f32),
            dma((STEPS, n)), dma((STEPS, n)), dma((STEPS, n)), dma((STEPS, n)),
            dma((STEPS, 8)), dma((STEPS, 8)),
        ],
        compiler_params=pltpu.CompilerParams(
            collective_id=0, has_side_effects=True, vmem_limit_bytes=56 * 1024 * 1024),
        name="shell_steps",
    )(positions, velocity, stiffness, route, route, paired, paired)


def solution(mesh):
    ngx, ngy = mesh.shape["gx"], mesh.shape["gy"]
    return jax.shard_map(
        functools.partial(local, ngx, ngy),
        mesh=mesh,
        in_specs=(
            P(None, "gx", "gy"),
            P(None, "gx", "gy"),
            P("gx", "gy"),
            P("gx", "gy"),
            P("gx", "gy", None, None),
        ),
        out_specs=(P(None, "gx", "gy"), P(None, "gx", "gy")),
        check_vma=False,
    )
```

time: 294 us -> 166 us (0.56)
  other arithmetic: 163 us -> 3.18 us
  Pallas kernels: 0 us -> 157 us
  starting transfers between devices: 44.3 us -> 0 us
  local copies, waits for them, and re-layouts: 42.9 us -> 4.79 us
  waiting for transfers between devices: 34.4 us -> 0 us
  matrix products: 5.33 us -> 0 us
    pallas_call x0 -> x1, Pallas kernels: none -> 157 us  [local(): pl.pallas_call(functools.partial(kernel, ngx, ngy, slots), out_shape=(sha...]
    reduce_sum x34 -> x0, other arithmetic: 98.9 us -> none  [the longest x16 63.1 us: pair_block(): return (jnp.sum(push, axis=3), -jnp.sum(push, axis=2))]
    all_to_all x4 -> x0, starting transfers between devices: 28.1 us -> none  [the longest x2 16.5 us: contact_force(): lax.all_to_all(sent, ('gx', 'gy'), split_axis=1, concat_axis=1, tiled=True)]
    ppermute x8 -> x0, waiting for transfers between devices: 27.8 us -> none  [the longest x4 27.8 us: extended(): lax.ppermute(tail, axis, [(i, (i + 1) % count) for i in range(ends)])]
    mul x36 -> x0, other arithmetic: 26.8 us -> none  [the longest x2 14.2 us: internal(): curve = laplace(wide) * inside[None]]
    add x8 -> x0, other arithmetic: 26 us -> none  [the longest x2 20.2 us: local(): positions = positions + time_step * velocity]
    ppermute x8 -> x0, starting transfers between devices: 16.2 us -> none  [the longest x4 11 us: extended(): lax.ppermute(tail, axis, [(i, (i + 1) % count) for i in range(ends)])]
    sub x32 -> x0, local copies, waits for them, and re-layouts: 13.1 us -> none  [pair_block(): offset = near[:, :, :, None] - far[:, :, None, :]]
  transfers between devices with their start and end apart: 12 -> 0, of which waited for: 4 -> 0; matrix products, arithmetic and copies ran while one was open for 16% -> 0% of each run, Pallas kernels for 0% -> 0%
where the time goes in v1:
time: 166 us
  Pallas kernels  157 us (95%)
  local copies, waits for them, and re-layouts  4.79 us (3%)
  other arithmetic  3.18 us (2%)
    pallas_call x1, Pallas kernels, local(): pl.pallas_call(functools.partial(kernel, ngx, ngy, slots), out_shape=(sha...  157 us
    unnamed x5, local copies, waits for them, and re-layouts  4.45 us

profile of v1, /device:TPU:0, one launch (start us, length us, event | category | flops | bytes accessed | tf_op | source)
XLA Modules:
  0.0 165.7 jit_solution(17838102265889618367)
XLA Ops:
  0.6 0.5 broadcast.109
  1.1 1.3 reduce.3
  2.5 1.3 compare_select_fusion.pair_s.pair_v
  3.7 0.1 reshape.117
  3.8 0.1 copy.11
  3.9 0.1 reshape.118
  4.0 0.1 ge.17
  4.1 0.6 add_select_fusion.route_s.route_v
  4.7 157.1 %shell_steps.1 = (f32[3,256,512]{2,1,0:T(8,128)}, f32[3,256,512]{2,1,0:T(8,128)}) custom-call(f32[3,256,512]{2,1,0:T(8,128)} %pos_ref.1, f32[3,256,512]{2,1,0:T(8,128)} %vel_ref.1, f32[256,512]{1,0:T(8,128)} %stiff_ref.1, s32[2,128]{1,0:T(2,128)} %add_select_fusion.route_s.route_v, s32[2,128]{1,0:T(2,128)} %add_select_fusion.route_s.route_v, ...), custom_call_target="tpu_custom_call" | custom-call | tf_op jit(solution)/shard_map/shell_steps/pallas_call | solution.py:339
  161.8 0.0 copy-start
  161.8 2.8 %copy.14 = f32[3,256,512]{2,1,0:T(8,128)} copy(f32[3,256,512]{2,1,0:T(8,128)} %get-tuple-element.6) | data formatting | bytes 3145728
  164.6 0.0 copy-done
  164.6 1.1 copy.15
  (2 shorter events, 0.0 us)
Async XLA Ops:
  161.8 2.8 %copy-start = (f32[3,256,512]{2,1,0:T(8,128)S(1)}, f32[3,256,512]{2,1,0:T(8,128)}, u32[]{:S(2)}) copy-start(f32[3,256,512]{2,1,0:T(8,128)} %get-tuple-element.7) | copy-start | bytes 4718596

commit v2 on v1

--- a/solution.py
+++ b/solution.py
@@ -17,8 +17,8 @@
 hardening = 0.1
 bend_gain = 0.02
 SCALE = math.sqrt(0.5 * math.log2(math.e))
-CHUNK = 32
-UNROLL = 4
+CHUNK = 64
+UNROLL = 16
 bf16 = jnp.bfloat16
 f32 = jnp.float32
 
@@ -97,34 +97,6 @@
                 col = jnp.maximum(col, 0)
                 for c in range(3):
                     put(k * 3 + c, blocks[col, c, pl.ds(row, 1), :] * filled)
-
-        def send_tiles(d, carry):
-            o = lax.rem(me + d, n)
-
-            def put(j, value):
-                sendbuf[step, o, pl.ds(j, 1), :] = value
-
-            fetch(o, put)
-            tile_copy(step, o, me).start()
-            return carry
-
-        lax.fori_loop(1, n, send_tiles, 0)
-
-        def put_own(j, value):
-            recv[step, me, pl.ds(j, 1), :] = value
-
-        fetch(me, put_own)
-
-        lane = lax.broadcasted_iota(jnp.int32, (rows, TILE), 1)
-        packed = jnp.zeros((rows, TILE), f32)
-        for c in range(3):
-            first = pltpu.roll(xpad[c, 8:8 + rows, 0:TILE], 2 * c, 1) if c else xpad[c, 8:8 + rows, 0:TILE]
-            last = pltpu.roll(xpad[c, 8:8 + rows, cols - TILE:cols], 10 + 2 * c, 1)
-            packed = jnp.where((lane == 2 * c) | (lane == 2 * c + 1), first, packed)
-            packed = jnp.where((lane == 8 + 2 * c) | (lane == 9 + 2 * c), last, packed)
-        turned = jnp.transpose(packed)
-        colsend[step, 0] = turned[0:8]
-        colsend[step, 1] = turned[8:16]
 
         top = pl.ds(8, 8)
         bottom = pl.ds(rows, 8)
@@ -146,7 +118,38 @@
                 device_id=where, device_id_type=MESH)
             for i, (src, dst, where) in enumerate(plans)
         ]
-        for copy in halos:
+        for copy in halos[2:]:
+            copy.start()
+
+        def send_tiles(d, carry):
+            o = lax.rem(me + d, n)
+
+            def put(j, value):
+                sendbuf[step, o, pl.ds(j, 1), :] = value
+
+            fetch(o, put)
+            tile_copy(step, o, me).start()
+            return carry
+
+        lax.fori_loop(1, n, send_tiles, 0)
+
+        def put_own(j, value):
+            recv[step, me, pl.ds(j, 1), :] = value
+
+        fetch(me, put_own)
+
+        lane = lax.broadcasted_iota(jnp.int32, (rows, TILE), 1)
+        packed = jnp.zeros((rows, TILE), f32)
+        for c in range(3):
+            first = pltpu.roll(xpad[c, 8:8 + rows, 0:TILE], 2 * c, 1) if c else xpad[c, 8:8 + rows, 0:TILE]
+            last = pltpu.roll(xpad[c, 8:8 + rows, cols - TILE:cols], 10 + 2 * c, 1)
+            packed = jnp.where((lane == 2 * c) | (lane == 2 * c + 1), first, packed)
+            packed = jnp.where((lane == 8 + 2 * c) | (lane == 9 + 2 * c), last, packed)
+        turned = jnp.transpose(packed)
+        colsend[step, 0] = turned[0:8]
+        colsend[step, 1] = turned[8:16]
+
+        for copy in halos[:2]:
             copy.start()
         for copy in halos:
             copy.wait()
@@ -204,7 +207,8 @@
                     stiff * pull[8:8 + CHUNK, 0:cols] - bend_gain * bend[8:8 + CHUNK, 0:cols])
             return carry
 
-        lax.fori_loop(0, rows // CHUNK, internal, 0)
+        half = rows // CHUNK // 2
+        lax.fori_loop(0, half, internal, 0)
 
         def tiles_in(d, carry):
             tile_copy(step, me, lax.rem(me + d, n)).wait_recv()
@@ -228,11 +232,14 @@
             out = out[0:8] + out[8:16]
             return out + pltpu.roll(out, 4, 0)
 
+        def slot_row(s):
+            return lax.rem(s, slots) * n + lax.div(s, slots)
+
         def pairs(g, carry):
             for u in range(UNROLL):
                 m = g * UNROLL + u
-                a = jnp.maximum(pair_s[0, m], 0)
-                b = jnp.maximum(pair_s[1, m], 0)
+                a = slot_row(jnp.maximum(pair_s[0, m], 0))
+                b = slot_row(jnp.maximum(pair_s[1, m], 0))
                 p = jnp.transpose(rec8[a])
                 q = rec8[b]
                 power = jnp.full((TILE, TILE), -2.0, f32)
@@ -257,6 +264,7 @@
         lax.fori_loop(0, number // UNROLL, pairs, 0)
 
         ids = lax.broadcasted_iota(jnp.int32, (total, number), 0)
+        ids = lax.rem(ids, n) * slots + lax.div(ids, n)
         hot = jnp.concatenate(
             [(ids == pair_v[0:1, :]).astype(f32), (ids == pair_v[1:2, :]).astype(f32)], axis=1).astype(bf16)
         summed = []
@@ -274,6 +282,7 @@
 
         lax.fori_loop(1, n, send_back, 0)
         back[step, me] = backsend[step, me]
+        lax.fori_loop(half, rows // CHUNK, internal, 0)
 
         def back_in(d, carry):
             back_copy(step, me, lax.rem(me + d, n)).wait_recv()
@@ -286,28 +295,21 @@
         parts = [jnp.concatenate([parts[c][i] for c in range(3)], axis=1) for i in range(3)]
         parts = jnp.concatenate(parts, axis=0)
 
-        def advance(chunk, carry):
-            r0 = pl.multiple_of(chunk * CHUNK, CHUNK)
-            span = pl.ds(r0, CHUNK)
-            ids = lax.broadcasted_iota(jnp.int32, (CHUNK, total), 0) + r0
-            in_row = ids == route_v[0:1, :]
-            for t in range(cols // TILE):
-                at = slice(t * TILE, (t + 1) * TILE)
-                hot = (in_row & (route_v[1:2, :] == t)).astype(f32).astype(bf16)
-                hot = jnp.concatenate([hot, hot, hot], axis=1)
-                contact = jnp.dot(hot, parts, preferred_element_type=f32)
-                for c in range(3):
-                    v = vel_out[c, span, at]
-                    push = force[c, span, at] + contact[:, c * TILE:(c + 1) * TILE]
-                    v = v + time_step * (push - damping * v)
-                    x = xpad[c, pl.ds(r0 + 8, CHUNK), at] + time_step * v
-                    vel_out[c, span, at] = v
-                    xpad[c, pl.ds(r0 + 8, CHUNK), at] = x
-                    blocks[t, c, span, :] = x
-                    pos_out[c, span, at] = x
-            return carry
-
-        lax.fori_loop(0, rows // CHUNK, advance, 0)
+        in_row = lax.broadcasted_iota(jnp.int32, (rows, total), 0) == route_v[0:1, :]
+        for t in range(cols // TILE):
+            at = slice(t * TILE, (t + 1) * TILE)
+            hot = (in_row & (route_v[1:2, :] == t)).astype(f32).astype(bf16)
+            hot = jnp.concatenate([hot, hot, hot], axis=1)
+            contact = jnp.dot(hot, parts, preferred_element_type=f32)
+            for c in range(3):
+                v = vel_out[c, :, at]
+                push = force[c, :, at] + contact[:, c * TILE:(c + 1) * TILE]
+                v = v + time_step * (push - damping * v)
+                x = xpad[c, 8:8 + rows, at] + time_step * v
+                vel_out[c, :, at] = v
+                xpad[c, 8:8 + rows, at] = x
+                blocks[t, c] = x
+                pos_out[c, :, at] = x
 
         def sent(d, carry):
             o = lax.rem(me + d, n)
@@ -330,7 +332,6 @@
     per_row = cols // TILE
     route = jnp.where(route >= 0, jnp.stack([route // per_row, route % per_row]), -1)
     paired = pair_tiles.reshape(2, -1)
-    paired = jnp.where(paired >= 0, (paired % slots) * n + paired // slots, -1)
     number = paired.shape[1]
     vmem = pl.BlockSpec(memory_space=pltpu.VMEM)
     smem = pl.BlockSpec(memory_space=pltpu.SMEM)

time: 166 us -> 116 us (0.70)
  Pallas kernels: 157 us -> 108 us
    pallas_call x1, Pallas kernels: 157 us -> 108 us  [local(): pl.pallas_call(functools.partial(kernel, ngx, ngy, slots), out_shape=(sha...]
where the time goes in v2:
time: 116 us
  Pallas kernels  108 us (93%)
  local copies, waits for them, and re-layouts  4.79 us (4%)
  other arithmetic  1.91 us (2%)
    pallas_call x1, Pallas kernels, local(): pl.pallas_call(functools.partial(kernel, ngx, ngy, slots), out_shape=(sha...  108 us
    unnamed x5, local copies, waits for them, and re-layouts  4.45 us

profile of v2, /device:TPU:0, one launch (start us, length us, event | category | flops | bytes accessed | tf_op | source)
XLA Modules:
  0.0 115.8 jit_solution(12491935936580704328)
XLA Ops:
  0.6 0.5 broadcast.100
  1.1 1.3 %reduce.3 = s32[128]{0:T(128)S(1)} reduce(s32[1,1,128]{2,1,0:T(1,128)} %param.8, s32[]{:T(128)} %broadcast.100), dimensions={0,1}, to_apply=%param.8.reduce_sub_computation.3 | reduce | bytes 1028 | tf_op args[3]
  2.5 0.1 reshape.117
  2.6 0.1 copy.11
  2.6 0.1 reshape.118
  2.7 0.1 ge.11
  2.8 0.6 add_select_fusion.route_s.route_v
  3.4 108.4 %shell_steps.1 = (f32[3,256,512]{2,1,0:T(8,128)}, f32[3,256,512]{2,1,0:T(8,128)}) custom-call(f32[3,256,512]{2,1,0:T(8,128)} %pos_ref.1, f32[3,256,512]{2,1,0:T(8,128)} %vel_ref.1, f32[256,512]{1,0:T(8,128)} %stiff_ref.1, s32[2,128]{1,0:T(2,128)} %add_select_fusion.route_s.route_v, s32[2,128]{1,0:T(2,128)} %add_select_fusion.route_s.route_v, ...), custom_call_target="tpu_custom_call" | custom-call | tf_op jit(solution)/shard_map/shell_steps/pallas_call | solution.py:340
  111.9 0.0 copy-start
  111.9 2.8 %copy.14 = f32[3,256,512]{2,1,0:T(8,128)} copy(f32[3,256,512]{2,1,0:T(8,128)} %get-tuple-element.6) | data formatting | bytes 3145728
  114.7 0.0 copy-done
  114.7 1.1 copy.15
  (2 shorter events, 0.0 us)
Async XLA Ops:
  111.9 2.8 %copy-start = (f32[3,256,512]{2,1,0:T(8,128)S(1)}, f32[3,256,512]{2,1,0:T(8,128)}, u32[]{:S(2)}) copy-start(f32[3,256,512]{2,1,0:T(8,128)} %get-tuple-element.7) | copy-start | bytes 4718596

commit v3 on v2

--- a/solution.py
+++ b/solution.py
@@ -32,7 +32,7 @@
 
 
 def kernel(ngx, ngy, slots, pos_ref, vel_ref, stiff_ref, route_s, route_v, pair_s, pair_v,
-           pos_out, vel_out, xpad, blocks, force, sendbuf, recv, backsend, back, rec8, aug, pairsum,
+           pos_out, vel_out, xpad, blocks, force, sendbuf, recv, backsend, back, rec8, aug, left_side, right_side, pairsum,
            colsend, colrecv, rowrecv, cornrecv,
            tile_send, tile_recv, back_send, back_recv, halo_send, halo_recv):
     n = ngx * ngy
@@ -76,13 +76,13 @@
 
     def tile_copy(step, o, source):
         return pltpu.make_async_remote_copy(
-            src_ref=sendbuf.at[step, o], dst_ref=recv.at[step, source],
+            src_ref=sendbuf.at[o], dst_ref=recv.at[step, source],
             send_sem=tile_send.at[step, o], recv_sem=tile_recv.at[step, source],
             device_id=place(o), device_id_type=MESH)
 
     def back_copy(step, o, source):
         return pltpu.make_async_remote_copy(
-            src_ref=backsend.at[step, o], dst_ref=back.at[step, source],
+            src_ref=backsend.at[o], dst_ref=back.at[step, source],
             send_sem=back_send.at[step, o], recv_sem=back_recv.at[step, source],
             device_id=place(o), device_id_type=MESH)
 
@@ -125,7 +125,7 @@
             o = lax.rem(me + d, n)
 
             def put(j, value):
-                sendbuf[step, o, pl.ds(j, 1), :] = value
+                sendbuf[o, pl.ds(j, 1), :] = value
 
             fetch(o, put)
             tile_copy(step, o, me).start()
@@ -221,9 +221,27 @@
 
         def split_slots(g, carry):
             at = pl.ds(g * 8, 8)
-            hi, mid, lo = split3(rec8[at])
-            second = mid.astype(f32) + pltpu.roll(lo.astype(f32), 4, 1)
-            aug[at] = jnp.concatenate([hi.astype(f32), second], axis=1).astype(bf16)
+            x = rec8[at]
+            hi, mid, lo = [part.astype(f32) for part in split3(x)]
+            second = mid + pltpu.roll(lo, 4, 1)
+            aug[at] = jnp.concatenate([hi, second], axis=1).astype(bf16)
+            norm = -1.0 - jnp.sum(x * x, axis=1, keepdims=True)
+            nh, nm, nl = [part.astype(f32) for part in split3(norm)]
+            row = lax.broadcasted_iota(jnp.int32, x.shape, 1)
+            zero = jnp.zeros_like(x)
+            ones = jnp.where(row < 6, 1.0, zero)
+            own = jnp.where(row == 0, nh, jnp.where(row == 1, nm, jnp.where(row == 2, nl, ones)))
+            other = jnp.where(row == 3, nh, jnp.where(row == 4, nm, jnp.where(row == 5, nl, ones)))
+            hi2, mid2, lo2 = 2.0 * hi, 2.0 * mid, 2.0 * lo
+
+            def both(upper, lower):
+                return upper + pltpu.roll(lower, 4, 1)
+
+            right_side[at] = jnp.concatenate(
+                [both(hi2, mid2), both(hi2, lo2), both(hi2, mid2), other], axis=1).astype(bf16)
+            whole = jnp.concatenate([both(hi, hi), both(mid, hi), both(lo, mid), own], axis=1)
+            for i in range(8):
+                left_side[g * 8 + i] = jnp.transpose(whole[i]).astype(bf16)
             return carry
 
         lax.fori_loop(0, total // 8, split_slots, 0)
@@ -240,12 +258,7 @@
                 m = g * UNROLL + u
                 a = slot_row(jnp.maximum(pair_s[0, m], 0))
                 b = slot_row(jnp.maximum(pair_s[1, m], 0))
-                p = jnp.transpose(rec8[a])
-                q = rec8[b]
-                power = jnp.full((TILE, TILE), -2.0, f32)
-                for c in range(3):
-                    d = p[:, c:c + 1] - q[c:c + 1, :]
-                    power = power - d * d
+                power = jnp.dot(left_side[a], right_side[b], preferred_element_type=f32)
                 w = jnp.exp2(power)
                 hi = w.astype(bf16)
                 lo = (w - hi.astype(f32)).astype(bf16)
@@ -274,14 +287,14 @@
         for c in range(3):
             push = (rec8[:, c, :] * summed[3] - summed[c]) * (1.0 / SCALE)
             for k in range(slots):
-                backsend[step, :, k * 3 + c, :] = push[k * n:(k + 1) * n]
+                backsend[:, k * 3 + c, :] = push[k * n:(k + 1) * n]
 
         def send_back(d, carry):
             back_copy(step, lax.rem(me + d, n), me).start()
             return carry
 
         lax.fori_loop(1, n, send_back, 0)
-        back[step, me] = backsend[step, me]
+        back[step, me] = backsend[me]
         lax.fori_loop(half, rows // CHUNK, internal, 0)
 
         def back_in(d, carry):
@@ -346,12 +359,14 @@
             pltpu.VMEM((3, rows + 16, cols + TILE), f32),
             pltpu.VMEM((cols // TILE, 3, rows, TILE), f32),
             pltpu.VMEM((3, rows, cols), f32),
+            pltpu.VMEM((n, slots * 3, TILE), f32),
             pltpu.VMEM((STEPS, n, slots * 3, TILE), f32),
-            pltpu.VMEM((STEPS, n, slots * 3, TILE), f32),
-            pltpu.VMEM((STEPS, n, slots * 3, TILE), f32),
+            pltpu.VMEM((n, slots * 3, TILE), f32),
             pltpu.VMEM((STEPS, n, slots * 3, TILE), f32),
             pltpu.VMEM((total, 8, TILE), f32),
             pltpu.VMEM((total, 16, TILE), bf16),
+            pltpu.VMEM((total, TILE, 32), bf16),
+            pltpu.VMEM((total, 32, TILE), bf16),
             pltpu.VMEM((2 * number, 8, TILE), f32),
             pltpu.VMEM((STEPS, 2, 8, rows), f32),
             pltpu.VMEM((STEPS, 2, 8, rows), f32),
@@ -361,7 +376,7 @@
             dma((STEPS, 8)), dma((STEPS, 8)),
         ],
         compiler_params=pltpu.CompilerParams(
-            collective_id=0, has_side_effects=True, vmem_limit_bytes=56 * 1024 * 1024),
+            collective_id=0, has_side_effects=True, vmem_limit_bytes=60 * 1024 * 1024),
         name="shell_steps",
     )(positions, velocity, stiffness, route, route, paired, paired)
 

time: 116 us -> 126 us (1.086)
  Pallas kernels: 108 us -> 119 us
    pallas_call x1, Pallas kernels: 108 us -> 119 us  [local(): pl.pallas_call(functools.partial(kernel, ngx, ngy, slots), out_shape=(sha...]
where the time goes in v3:
time: 126 us
  Pallas kernels  119 us (94%)
  local copies, waits for them, and re-layouts  4.79 us (4%)
  other arithmetic  1.91 us (2%)
    pallas_call x1, Pallas kernels, local(): pl.pallas_call(functools.partial(kernel, ngx, ngy, slots), out_shape=(sha...  119 us
    unnamed x5, local copies, waits for them, and re-layouts  4.45 us

profile of v3, /device:TPU:0, one launch (start us, length us, event | category | flops | bytes accessed | tf_op | source)
XLA Modules:
  0.0 125.9 jit_solution(16646668265508738196)
XLA Ops:
  0.6 0.5 broadcast.100
  1.1 1.3 %reduce.3 = s32[128]{0:T(128)S(1)} reduce(s32[1,1,128]{2,1,0:T(1,128)} %param.8, s32[]{:T(128)} %broadcast.100), dimensions={0,1}, to_apply=%param.8.reduce_sub_computation.3 | reduce | bytes 1028 | tf_op args[3]
  2.5 0.1 reshape.117
  2.6 0.1 copy.11
  2.6 0.1 reshape.118
  2.7 0.1 ge.11
  2.8 0.6 add_select_fusion.route_s.route_v
  3.4 118.5 %shell_steps.1 = (f32[3,256,512]{2,1,0:T(8,128)}, f32[3,256,512]{2,1,0:T(8,128)}) custom-call(f32[3,256,512]{2,1,0:T(8,128)} %pos_ref.1, f32[3,256,512]{2,1,0:T(8,128)} %vel_ref.1, f32[256,512]{1,0:T(8,128)} %stiff_ref.1, s32[2,128]{1,0:T(2,128)} %add_select_fusion.route_s.route_v, s32[2,128]{1,0:T(2,128)} %add_select_fusion.route_s.route_v, ...), custom_call_target="tpu_custom_call" | custom-call | tf_op jit(solution)/shard_map/shell_steps/pallas_call | solution.py:353
  121.9 0.0 copy-start
  121.9 2.8 %copy.14 = f32[3,256,512]{2,1,0:T(8,128)} copy(f32[3,256,512]{2,1,0:T(8,128)} %get-tuple-element.6) | data formatting | bytes 3145728
  124.7 0.0 copy-done
  124.7 1.1 copy.15
  (2 shorter events, 0.0 us)
Async XLA Ops:
  121.9 2.8 %copy-start = (f32[3,256,512]{2,1,0:T(8,128)S(1)}, f32[3,256,512]{2,1,0:T(8,128)}, u32[]{:S(2)}) copy-start(f32[3,256,512]{2,1,0:T(8,128)} %get-tuple-element.7) | copy-start | bytes 4718596

commit v4 on v2

--- a/solution.py
+++ b/solution.py
@@ -19,6 +19,7 @@
 SCALE = math.sqrt(0.5 * math.log2(math.e))
 CHUNK = 64
 UNROLL = 16
+BLOCK = 32
 bf16 = jnp.bfloat16
 f32 = jnp.float32
 
@@ -62,6 +63,7 @@
     vel_out[...] = vel_ref[...]
     rec8[...] = jnp.zeros_like(rec8)
     rec8[:, 3, :] = jnp.ones((total, TILE), f32)
+    pairsum[number:2 * number] = jnp.zeros((number, 8, TILE), f32)
 
     pl.semaphore_wait(barrier, n - 1)
 
@@ -242,23 +244,27 @@
                 b = slot_row(jnp.maximum(pair_s[1, m], 0))
                 p = jnp.transpose(rec8[a])
                 q = rec8[b]
-                power = jnp.full((TILE, TILE), -2.0, f32)
+                his, los = [], []
+                far = [jnp.zeros((8, TILE), f32) for c in range(3)]
+                for r in range(0, TILE, BLOCK):
+                    d = [p[r:r + BLOCK, c:c + 1] - q[c:c + 1, :] for c in range(3)]
+                    w = jnp.exp2(-2.0 - (d[0] * d[0] + d[1] * d[1] + d[2] * d[2]))
+                    hi = w.astype(bf16)
+                    his.append(hi)
+                    los.append((w - hi.astype(f32)).astype(bf16))
+                    for c in range(3):
+                        push = w * d[c]
+                        for e in range(0, BLOCK, 8):
+                            far[c] = far[c] + push[e:e + 8]
+                qb = aug[b]
+                qb = jnp.concatenate([qb, qb], axis=1)
+                weights = jnp.concatenate(
+                    [jnp.concatenate(his, axis=0), jnp.concatenate(los, axis=0)], axis=1)
+                near = lax.dot_general(
+                    qb, weights, (((1,), (1,)), ((), ())), preferred_element_type=f32)
+                pairsum[m] = sums(near)
                 for c in range(3):
-                    d = p[:, c:c + 1] - q[c:c + 1, :]
-                    power = power - d * d
-                w = jnp.exp2(power)
-                hi = w.astype(bf16)
-                lo = (w - hi.astype(f32)).astype(bf16)
-                pa = aug[a]
-                qb = aug[b]
-                pa = jnp.concatenate([pa, pa], axis=1)
-                qb = jnp.concatenate([qb, qb], axis=1)
-                far = jnp.dot(pa, jnp.concatenate([hi, lo], axis=0), preferred_element_type=f32)
-                near = lax.dot_general(
-                    qb, jnp.concatenate([hi, lo], axis=1), (((1,), (1,)), ((), ())),
-                    preferred_element_type=f32)
-                pairsum[m] = sums(near)
-                pairsum[number + m] = sums(far)
+                    pairsum[number + m, c:c + 1, :] = jnp.sum(far[c], axis=0, keepdims=True)
             return carry
 
         lax.fori_loop(0, number // UNROLL, pairs, 0)

time: 116 us -> 119 us (1.026)
  Pallas kernels: 108 us -> 112 us
    pallas_call x1, Pallas kernels: 108 us -> 112 us  [local(): pl.pallas_call(functools.partial(kernel, ngx, ngy, slots), out_shape=(sha...]
where the time goes in v4:
time: 119 us
  Pallas kernels  112 us (94%)
  local copies, waits for them, and re-layouts  4.79 us (4%)
  other arithmetic  1.91 us (2%)
    pallas_call x1, Pallas kernels, local(): pl.pallas_call(functools.partial(kernel, ngx, ngy, slots), out_shape=(sha...  112 us
    unnamed x5, local copies, waits for them, and re-layouts  4.45 us

profile of v4, /device:TPU:0, one launch (start us, length us, event | category | flops | bytes accessed | tf_op | source)
XLA Modules:
  0.0 119.2 jit_solution(4195432577319696938)
XLA Ops:
  0.6 0.5 broadcast.100
  1.1 1.3 %reduce.3 = s32[128]{0:T(128)S(1)} reduce(s32[1,1,128]{2,1,0:T(1,128)} %param.8, s32[]{:T(128)} %broadcast.100), dimensions={0,1}, to_apply=%param.8.reduce_sub_computation.3 | reduce | bytes 1028 | tf_op args[3]
  2.5 0.1 reshape.117
  2.6 0.1 copy.11
  2.6 0.1 reshape.118
  2.7 0.1 ge.11
  2.8 0.6 add_select_fusion.route_s.route_v
  3.4 111.8 %shell_steps.1 = (f32[3,256,512]{2,1,0:T(8,128)}, f32[3,256,512]{2,1,0:T(8,128)}) custom-call(f32[3,256,512]{2,1,0:T(8,128)} %pos_ref.1, f32[3,256,512]{2,1,0:T(8,128)} %vel_ref.1, f32[256,512]{1,0:T(8,128)} %stiff_ref.1, s32[2,128]{1,0:T(2,128)} %add_select_fusion.route_s.route_v, s32[2,128]{1,0:T(2,128)} %add_select_fusion.route_s.route_v, ...), custom_call_target="tpu_custom_call" | custom-call | tf_op jit(solution)/shard_map/shell_steps/pallas_call | solution.py:346
  115.3 0.0 copy-start
  115.3 2.8 %copy.14 = f32[3,256,512]{2,1,0:T(8,128)} copy(f32[3,256,512]{2,1,0:T(8,128)} %get-tuple-element.6) | data formatting | bytes 3145728
  118.1 0.0 copy-done
  118.1 1.1 copy.15
  (2 shorter events, 0.0 us)
Async XLA Ops:
  115.3 2.8 %copy-start = (f32[3,256,512]{2,1,0:T(8,128)S(1)}, f32[3,256,512]{2,1,0:T(8,128)}, u32[]{:S(2)}) copy-start(f32[3,256,512]{2,1,0:T(8,128)} %get-tuple-element.7) | copy-start | bytes 4718596
